TPU v7x, 128 devices: a whole 4x4x4 slice. The times are simulated.
128 devices in a mesh: frame: 32 (over x, z_lo, y), sp: 4 (over z_hi, core).
Axes of the slice: x: 4, y: 4, z: 4 (z_hi: 2, z_lo: 2; z = z_hi * 2 + z_lo), core: 2. Of those that a mesh axis runs over, the one named last changes fastest.
Arguments:
- frames_in: bfloat16 [32, 64, 36, 640], P('frame', 'sp'), may hold values from -6 to 6
- reference_rows: bfloat16 [2304, 640], P(('frame', 'sp')), may hold values from -60 to 60
- norm_conv: float32 [640], replicated, may hold values from 0.1 to 1.9
- conv_weight: bfloat16 [3, 3, 640, 640], replicated, may hold values from -0.078125 to 0.078125
- norm_attn: float32 [640], replicated, may hold values from 0.1 to 1.9
- spatial_qkv: bfloat16 [3, 640, 640], replicated, may hold values from -2 to 2
- spatial_out: bfloat16 [640, 640], replicated, may hold values from -0.25 to 0.25
- time_weight: bfloat16 [3, 640, 640], replicated, may hold values from -0.125 to 0.125
- norm_time: float32 [640], replicated, may hold values from 0.1 to 1.9
- temporal_qkv: bfloat16 [3, 640, 640], replicated, may hold values from -1 to 1
- temporal_out: bfloat16 [640, 640], replicated, may hold values from -0.25 to 0.25
Outputs:
- block_out: bfloat16 [32, 64, 36, 640], P('frame', 'sp')
All inputs are finite; a program needn't handle non-finite values.
Results may differ from a plain program's by a relative error of at most 0.018.
Values may be sent and summed in bfloat16 or wider, within the bound.
A program may use at most 128 MiB of HBM per device.

v0:
```python
import functools

import jax
import jax.numpy as jnp
from jax import lax
from jax.experimental import pallas as pl
from jax.experimental.pallas import tpu as pltpu
from jax.sharding import PartitionSpec as P

MESH = pl.DeviceIdType.MESH
BF = jnp.bfloat16
F32 = jnp.float32
C = 640
HEADS = 8
D = 80
MINE = 4
OWN = MINE * D
ROWS = 16
W = 36
PITCH = 40
CELLS = 576
CHIP = 1152
FRAMES = 32
CHUNKS = 3
SLOT = 8
USED = 6
PART = CELLS // CHUNKS
WIDE = FRAMES * SLOT
SCALE = (D ** -0.5) * 1.4426950408889634


def dot(a, b):
    return jnp.dot(a, b, preferred_element_type=F32)


def dot_nt(a, b):
    return lax.dot_general(a, b, (((1,), (1,)), ((), ())), preferred_element_type=F32)


def dot_tn(a, b):
    return lax.dot_general(a, b, (((0,), (0,)), ((), ())), preferred_element_type=F32)


def layer_norm(values, gain):
    mean = jnp.mean(values, axis=-1, keepdims=True)
    centred = values - mean
    spread = jnp.mean(centred * centred, axis=-1, keepdims=True)
    return centred * lax.rsqrt(spread + 1e-05) * gain


def kernel(
    frames, refs, norm_conv, conv_w, norm_attn, sqkv, sout, time_w, norm_time, tqkv, tout,
    out,
    xin, wc, wsq, wso,
    filt, grid, mid,
    rblk, allx, wqt, wvt, wkp, qt, kk, vt, acc, mx, al, s0, s1,
    part, psend, precv,
    asend, arecv, brecv, tgrid, tatt, final, oblk,
    lsem, hs, hr, cs, cr, p1s, p1r, p2s, p2r, xs, xr, ps, pr, a_s, a_r, b_s, b_r,
):
    f = lax.axis_index("frame")
    s = lax.axis_index("sp")
    x = f // 8
    y = f % 4
    z = (s // 2) * 2 + (f // 4) % 2
    core = s % 2
    zc = z * 2 + core

    def dev(px, py, pz, pc):
        px, py, pz = lax.rem(px, 4), lax.rem(py, 4), lax.rem(pz, 4)
        return ((px * 2 + pz % 2) * 4 + py, (pz // 2) * 2 + pc)

    sib = (f, (s // 2) * 2 + 1 - core)
    far = (f, lax.rem(s + 2, 4))

    loads = [
        (frames.at[0], xin.at[pl.ds(1, ROWS)]),
        (refs, rblk.at[zc]),
        (sqkv, wsq),
    ]
    loads += [(conv_w.at[a, b], wc.at[b, pl.ds(a * C, C)]) for b in range(3) for a in range(3)]
    loads += [(sout, wso)]
    loads += [(time_w.at[a], wc.at[0, pl.ds(a * C, C)]) for a in range(3)]
    loads += [(tqkv.at[a], wc.at[1, pl.ds(a * C, C)]) for a in range(3)]
    loads += [(tout, wc.at[2, pl.ds(0, C)])]
    local = [pltpu.make_async_copy(a, b, lsem.at[i]) for i, (a, b) in enumerate(loads)]
    for cp in local[:13]:
        cp.start()

    bar = pltpu.get_barrier_semaphore()
    column = [(dz, dc) for dz in range(4) for dc in range(2) if dz + dc > 0]

    def col_dev(dz, dc):
        return dev(x, y, z + dz, lax.rem(core + dc, 2))

    others = [(dz, dc) for dz, dc in column if not (dz == 0 and dc == 0)]
    for dz, dc in others:
        pl.semaphore_signal(bar, inc=1, device_id=col_dev(dz, dc), device_id_type=MESH)

    def greet(i, _):
        pl.semaphore_signal(
            bar, inc=1, device_id=(lax.rem(f + i, FRAMES), s), device_id_type=MESH
        )
        return 0

    lax.fori_loop(1, FRAMES, greet, 0)
    pl.semaphore_wait(bar, len(others) + FRAMES - 1)

    def remote(src, dst, send, recv, to):
        return pltpu.make_async_remote_copy(
            src_ref=src, dst_ref=dst, send_sem=send, recv_sem=recv, device_id=to, device_id_type=MESH
        )

    up = remote(frames.at[0, 0], xin.at[ROWS + 1], hs.at[0], hr.at[0], (f, jnp.maximum(s - 1, 0)))
    down = remote(frames.at[0, ROWS - 1], xin.at[0], hs.at[1], hr.at[1], (f, jnp.minimum(s + 1, 3)))

    @pl.when(s > 0)
    def _():
        up.start()

    @pl.when(s < 3)
    def _():
        down.start()

    col = [
        remote(refs, rblk.at[zc], cs.at[i], cr.at[i], col_dev(dz, dc))
        for i, (dz, dc) in enumerate(column)
    ]
    for cp in col:
        cp.start()

    local[2].wait()
    pick = (
        lax.broadcasted_iota(jnp.int32, (OWN, C), 1)
        == lax.broadcasted_iota(jnp.int32, (OWN, C), 0) + OWN * core
    ).astype(F32).astype(BF)
    wqt[...] = dot_nt(pick, wsq[0]).astype(BF)
    wvt[...] = dot_nt(pick, wsq[2]).astype(BF)
    lane = lax.broadcasted_iota(jnp.int32, (C, MINE * 128), 1)
    row = lax.broadcasted_iota(jnp.int32, (C, MINE * 128), 0)
    spread = jnp.where(
        jnp.logical_and(lane % 128 < D, row == OWN * core + (lane // 128) * D + lane % 128), 1.0, 0.0
    ).astype(BF)
    wkp[...] = dot(wsq[1], spread).astype(BF)
    vt[:, D:, :] = jnp.where(
        lax.broadcasted_iota(jnp.int32, (MINE, 16, CHIP), 1) == 0, 1.0, 0.0
    ).astype(BF)

    filt[...] = jnp.zeros_like(filt)
    gain_conv = norm_conv[...]

    def activate(k, keep=None):
        v = layer_norm(xin[k].astype(F32), gain_conv)
        v = v / (1.0 + jnp.exp(-v))
        filt[pl.ds(pl.multiple_of(PITCH * k, 8), W), :] = v

    local[0].wait()

    def activate_step(k, _):
        activate(k)
        return 0

    lax.fori_loop(1, ROWS + 1, activate_step, 0)

    local[1].wait()
    for cp in col:
        cp.wait()
    for i in range(8):
        mid[pl.ds(18 * i, 18), :] = rblk[i].astype(F32)
    mine = jnp.int32(1) + x // 2
    allx[mine, lax.rem(x, 2), y] = mid[:144, :].astype(BF)

    def share(first, count):
        return pl.ds(pl.multiple_of(first, 16), count)

    half = share(64 * core, 80)
    home = allx.at[mine, lax.rem(x, 2), y, half]
    p1x = [remote(home, home, p1s.at[i - 1], p1r.at[i - 1], dev(x + i, y, z, core)) for i in (1, 2, 3)]
    p1y = [remote(home, home, p1s.at[i - 1], p1r.at[i - 1], dev(x, y + i, z, core)) for i in (1, 2, 3)]
    line_x = allx.at[pl.ds(1, 2), :, y, half]
    line_y = allx.at[mine, lax.rem(x, 2), :, half]
    p2y = [remote(line_x, line_x, p2s.at[i - 1], p2r.at[i - 1], dev(x, y + i, z, core)) for i in (1, 2, 3)]
    p2x = [remote(line_y, line_y, p2s.at[i - 1], p2r.at[i - 1], dev(x + i, y, z, core)) for i in (1, 2, 3)]

    def by_core(on0, on1, act):
        @pl.when(core == 0)
        def _():
            for cp in on0:
                act(cp)

        @pl.when(core == 1)
        def _():
            for cp in on1:
                act(cp)

    by_core(p1x, p1y, lambda cp: cp.start())

    @pl.when(s > 0)
    def _():
        down.wait_recv()
        activate(0)

    @pl.when(s < 3)
    def _():
        up.wait_recv()
        activate(ROWS + 1)

    @pl.when(s > 0)
    def _():
        up.wait_send()

    @pl.when(s < 3)
    def _():
        down.wait_send()

    def lay(k, _):
        to = pl.ds(pl.multiple_of(80 * k, 16), 80)
        for a in range(3):
            grid[to, a * C : (a + 1) * C] = filt[
                pl.ds(pl.multiple_of(80 * k + PITCH * a, 8), 80), :
            ].astype(BF)
        return 0

    lax.fori_loop(0, 8, lay, 0)
    zero = jnp.zeros((8, C), F32)
    zconv = (s0, s1, filt)
    for i in range(3, 12):
        local[i].wait()
    for b in range(3):
        zconv[b][:8, :C] = zero
        zconv[b][8 + 640 : 16 + 640, :C] = zero
        zconv[b][8 : 8 + 640, :C] = dot(grid[...], wc[b])
        if b == 0:
            by_core(p1x, p1y, lambda cp: cp.wait())
            by_core(p2y, p2x, lambda cp: cp.start())
    for cp in local[13:]:
        cp.start()
    gain_attn = norm_attn[...]
    for k in range(ROWS):
        at = 8 + PITCH * k
        total = (
            s0[at - 1 : at - 1 + W, :C] + s1[at : at + W, :C] + filt[at + 1 : at + 1 + W, :]
        )
        middle = (xin[k + 1].astype(F32) + total).astype(BF).astype(F32)
        mid[W * k : W * k + W, :] = middle
        final[W * k : W * k + W, :] = layer_norm(middle, gain_attn)
    allx[0, 0] = final[...].reshape(4, 144, C).astype(BF)

    to_sib = remote(allx.at[0, 0], allx.at[0, 1], xs.at[0], xr.at[0], sib)
    to_far = remote(allx.at[0, 0], allx.at[3, 0], xs.at[1], xr.at[1], far)
    to_far.start()
    to_sib.start()
    relay = remote(allx.at[3, 0], allx.at[3, 1], xs.at[2], xr.at[2], sib)
    give = allx.at[pl.ds(1, 2), :, :, share(80 * core, 64)]
    ref_swap = remote(give, give, xs.at[3], xr.at[3], sib)

    acc[...] = jnp.zeros_like(acc)
    mx[...] = jnp.full_like(mx, -1e30)
    to_sib.wait_recv()
    qall = dot_nt(wqt[...], allx[0].reshape(CHIP, C)) * SCALE
    qt[...] = qall.astype(BF)

    def scores(h, sref):
        sc = dot(kk[h][:, :D], qt[h * D : (h + 1) * D, :])
        sref[...] = sc
        old = mx[h]
        new = jnp.maximum(old, jnp.max(sc, axis=0, keepdims=True))
        mx[h] = new
        al[h] = jnp.exp2(old - new)

    def weigh(h, sref):
        p = jnp.exp2(sref[...] - mx[h]).astype(BF)
        acc[h] = acc[h] * al[h] + dot(vt[h], p)

    def attend(c, _):
        @pl.when(c == 1)
        def _():
            ref_swap.wait_recv()

        @pl.when(c == 2)
        def _():
            to_far.wait_recv()
            relay.start()

        @pl.when(c == 3)
        def _():
            relay.wait_recv()

        rows = allx[c].reshape(CHIP, C)
        keys = dot(rows, wkp[...])
        vals = dot_nt(wvt[...], rows)
        for h in range(MINE):
            kk[h] = keys[:, h * 128 : (h + 1) * 128].astype(BF)
            vt[h, :D, :] = vals[h * D : (h + 1) * D, :].astype(BF)
        scores(0, s0)
        weigh(0, s0)
        scores(1, s1)
        weigh(1, s1)
        scores(2, s0)

        @pl.when(c == 0)
        def _():
            by_core(p2y, p2x, lambda cp: cp.wait())
            ref_swap.start()

        weigh(2, s0)
        scores(3, s1)
        weigh(3, s1)
        return 0

    lax.fori_loop(0, 4, attend, 0)
    to_sib.wait_send()
    to_far.wait_send()
    relay.wait_send()
    ref_swap.wait_send()
    for i in range(12, len(local)):
        local[i].wait()

    for h in range(MINE):
        qt[h * D : (h + 1) * D, :] = (acc[h, :D, :] / acc[h, D : D + 1, :]).astype(BF)
    wout = wso[pl.ds(pl.multiple_of(OWN * core, 16), OWN), :]
    part[...] = dot_tn(qt[...], wout)
    psend[...] = part[CELLS:, :].astype(BF)
    swaps = [
        remote(
            psend.at[pl.ds(PART * j, PART)], precv.at[pl.ds(PART * j, PART)], ps.at[j], pr.at[j], sib
        )
        for j in range(CHUNKS)
    ]
    for cp in swaps:
        cp.start()

    wide_row = lax.broadcasted_iota(jnp.int32, (WIDE, PART), 0)
    part_row = lax.broadcasted_iota(jnp.int32, (WIDE, PART), 1)
    fan = jnp.where(
        jnp.logical_and(wide_row % SLOT < USED, part_row == (wide_row // SLOT) * USED + wide_row % SLOT),
        1.0, 0.0,
    ).astype(BF)

    def to_all(src, dst, send, recv, j):
        def go(i, _):
            peer = lax.rem(f + i, FRAMES)
            remote(src.at[j, peer], dst.at[j, f], send.at[j, peer], recv.at[j, f], (peer, s)).start()
            return 0

        lax.fori_loop(1, FRAMES, go, 0)
        dst[j, f] = src[j, f]

    def from_all(src, dst, send, recv, j):
        def go(i, _):
            peer = lax.rem(f + i, FRAMES)
            remote(src.at[j, peer], dst.at[j, peer], send.at[j, peer], recv.at[j, peer], (peer, s)).wait()
            return 0

        lax.fori_loop(1, FRAMES, go, 0)

    def depart(j, _):
        @pl.when(j == 0)
        def _():
            swaps[0].wait()

        @pl.when(j == 1)
        def _():
            swaps[1].wait()

        @pl.when(j == 2)
        def _():
            swaps[2].wait()

        at = pl.ds(pl.multiple_of(PART * j, 16), PART)
        after = (mid[at, :] + part[at, :] + precv[at, :].astype(F32)).astype(BF)
        asend[j] = dot(fan, after).reshape(FRAMES, SLOT, C).astype(BF)
        to_all(asend, arecv, a_s, a_r, j)
        return 0

    lax.fori_loop(0, CHUNKS, depart, 0)

    gain_time = norm_time[...]
    same = (
        lax.broadcasted_iota(jnp.int32, (WIDE, WIDE), 0) % SLOT
        == lax.broadcasted_iota(jnp.int32, (WIDE, WIDE), 1) % SLOT
    )
    def through_time(j, _):
        from_all(asend, arecv, a_s, a_r, j)
        block = arecv[j].astype(F32).reshape(WIDE, C)
        tgrid[:, :C] = jnp.concatenate([zero, block[:-SLOT]], axis=0).astype(BF)
        tgrid[:, C : 2 * C] = block.astype(BF)
        tgrid[:, 2 * C :] = jnp.concatenate([block[SLOT:], zero], axis=0).astype(BF)
        timed = (block + dot(tgrid[...], wc[0])).astype(BF).astype(F32)
        tn = layer_norm(timed, gain_time).astype(BF)
        q = (dot(tn, wc[1, 0 * C : 1 * C, :]) * SCALE).astype(BF)
        k = dot(tn, wc[1, 1 * C : 2 * C, :]).astype(BF)
        v = dot(tn, wc[1, 2 * C : 3 * C, :]).astype(BF)
        for h in range(HEADS):
            lo, hi = (h * D) // 128 * 128, -(-((h + 1) * D) // 128) * 128
            ln = lax.broadcasted_iota(jnp.int32, (1, hi - lo), 1) + lo
            inside = jnp.logical_and(ln >= h * D, ln < (h + 1) * D)
            qh = q[:, lo:hi] * jnp.where(inside, 1.0, 0.0).astype(BF)
            sc = jnp.where(same, dot_nt(qh, k[:, lo:hi]), -1e30)
            e = jnp.exp2(sc - jnp.max(sc, axis=1, keepdims=True))
            total = jnp.sum(e, axis=1, keepdims=True)
            o = dot(e.astype(BF), v[:, lo:hi]) / total
            if h == 0:
                tatt[:, lo:hi] = o
            else:
                tatt[:, lo:hi] = jnp.where(inside, o, tatt[:, lo:hi])
        res = timed + dot(tatt[...].astype(BF), wc[2, :C, :])
        asend[j] = res.reshape(FRAMES, SLOT, C).astype(BF)
        to_all(asend, brecv, b_s, b_r, j)
        return 0

    lax.fori_loop(0, CHUNKS, through_time, 0)

    def arrive(j, _):
        from_all(asend, brecv, b_s, b_r, j)
        got = brecv[j].astype(F32).reshape(WIDE, C).astype(BF)
        final[pl.ds(pl.multiple_of(PART * j, 16), PART), :] = dot_tn(fan, got)
        return 0

    lax.fori_loop(0, CHUNKS, arrive, 0)
    for k in range(ROWS):
        oblk[k] = final[W * k : W * k + W, :].astype(BF)
    done = pltpu.make_async_copy(oblk, out.at[0], lsem.at[0])
    done.start()
    done.wait()


def block(
    frames_in, reference_rows, norm_conv, conv_weight, norm_attn, spatial_qkv, spatial_out,
    time_weight, norm_time, temporal_qkv, temporal_out,
):
    hbm = pl.BlockSpec(memory_space=pl.ANY)
    vm = pl.BlockSpec(memory_space=pltpu.VMEM)
    v = pltpu.VMEM
    dma = pltpu.SemaphoreType.DMA
    scratch = [
        v((ROWS + 2, W, C), BF), v((3, 3 * C, C), BF), v((3, C, C), BF), v((C, C), BF),
        v((18 * PITCH, C), F32), v((640, 3 * C), BF), v((CELLS, C), F32),
        v((8, 18, C), BF), v((4, 2, 4, 144, C), BF), v((OWN, C), BF), v((OWN, C), BF),
        v((C, MINE * 128), BF), v((OWN, CHIP), BF), v((MINE, CHIP, 128), BF), v((MINE, 96, CHIP), BF),
        v((MINE, 96, CHIP), F32), v((MINE, 1, CHIP), F32), v((MINE, 1, CHIP), F32),
        v((CHIP, CHIP), F32), v((CHIP, CHIP), F32),
        v((CHIP, C), F32), v((CELLS, C), BF), v((CELLS, C), BF),
        v((CHUNKS, FRAMES, SLOT, C), BF), v((CHUNKS, FRAMES, SLOT, C), BF),
        v((CHUNKS, FRAMES, SLOT, C), BF),
        v((WIDE, 3 * C), BF), v((WIDE, C), F32), v((CELLS, C), F32), v((ROWS, W, C), BF),
        dma((20,)), dma((2,)), dma((2,)), dma((7,)), dma((7,)),
        dma((3,)), dma((3,)), dma((3,)), dma((3,)), dma((4,)), dma((4,)), dma((3,)), dma((3,)),
        dma((CHUNKS, FRAMES)), dma((CHUNKS, FRAMES)), dma((CHUNKS, FRAMES)), dma((CHUNKS, FRAMES)),
    ]
    return pl.pallas_call(
        kernel,
        out_shape=jax.ShapeDtypeStruct(frames_in.shape, BF),
        in_specs=[hbm, hbm, vm, hbm, vm, hbm, hbm, hbm, vm, hbm, hbm],
        out_specs=hbm,
        scratch_shapes=scratch,
        compiler_params=pltpu.CompilerParams(
            collective_id=0, has_side_effects=True, vmem_limit_bytes=62 * 2**20
        ),
    )(
        frames_in, reference_rows, norm_conv.reshape(1, C), conv_weight, norm_attn.reshape(1, C),
        spatial_qkv, spatial_out, time_weight, norm_time.reshape(1, C), temporal_qkv, temporal_out,
    )


def solution(mesh):
    rep = P()
    in_specs = (P("frame", "sp", None, None), P(("frame", "sp"), None)) + (rep,) * 9
    return jax.shard_map(
        block, mesh=mesh, in_specs=in_specs, out_specs=P("frame", "sp", None, None), check_vma=False
    )
```

profile of v0, /device:TPU:1, one launch (start us, length us, event | category | flops | bytes accessed | tf_op | source)
XLA Modules:
  0.0 104.6 jit_solution(6273711497700041722)
XLA Ops:
  0.0 1.3 %reshape.9.norm_conv = f32[1,640]{1,0:T(1,128)} reshape(f32[640]{0:T(1024)} %param.13) | data formatting | bytes 5120 | tf_op jit(solution)/shard_map/reshape | solution.py:461
  1.3 1.3 %reshape.10.norm_attn = f32[1,640]{1,0:T(1,128)} reshape(f32[640]{0:T(1024)} %param.15) | data formatting | bytes 5120 | tf_op jit(solution)/shard_map/reshape | solution.py:461
  2.5 1.3 %reshape.11.norm_time = f32[1,640]{1,0:T(1,128)} reshape(f32[640]{0:T(1024)} %param.19) | data formatting | bytes 5120 | tf_op jit(solution)/shard_map/reshape | solution.py:462
  3.8 2.1 %copy.12.frames = bf16[1,16,36,640]{3,2,1,0:T(8,128)(2,1)} copy(bf16[1,16,36,640]{3,1,2,0:T(8,128)(2,1)} %param.11) | data formatting | bytes 1474560 | tf_op args[0]
  6.0 96.6 %shard_map.109 = bf16[1,16,36,640]{3,2,1,0:T(8,128)(2,1)} custom-call(bf16[1,16,36,640]{3,2,1,0:T(8,128)(2,1)} %copy.12.frames, bf16[18,640]{1,0:T(8,128)(2,1)} %refs.1, f32[1,640]{1,0:T(1,128)} %reshape.9.norm_conv, bf16[3,3,640,640]{3,2,1,0:T(8,128)(2,1)} %conv_w.1, f32[1,640]{1,0:T(1,128)} %reshape.10.norm_attn, bf16[3,640,640]{2,1,0:T(8,128)(2,1)} %sqkv.1, ...), custom_call_target="tpu_custom_call" | custom-call | tf_op jit(solution)/shard_map/pallas_call | solution.py:451
  102.5 2.1 %copy.13 = bf16[1,16,36,640]{3,1,2,0:T(8,128)(2,1)} copy(bf16[1,16,36,640]{3,2,1,0:T(8,128)(2,1)} %shard_map.109) | data formatting | bytes 1474560 | tf_op jit(solution)/shard_map/pallas_call | solution.py:451
where the time goes:
time: 106 us; the launch traced here: 105 us
  Pallas kernels  96.6 us (91%)
  local copies, waits for them, and re-layouts  8.05 us (8%)
    pallas_call x1, Pallas kernels, block(): pl.pallas_call(kernel, out_shape=jax.ShapeDtypeStruct(frames_in.shape, BF...  96.6 us
    unnamed x1, local copies, waits for them, and re-layouts  2.15 us

commit v1 on v0

v1 whole, which is shorter than its diff:
```python
import functools

import jax
import jax.numpy as jnp
from jax import lax
from jax.experimental import pallas as pl
from jax.experimental.pallas import tpu as pltpu
from jax.sharding import PartitionSpec as P

MESH = pl.DeviceIdType.MESH
BF = jnp.bfloat16
F32 = jnp.float32
C = 640
HEADS = 8
D = 80
MINE = 4
OWN = MINE * D
ROWS = 16
W = 36
CELLS = 576
CHIP = 1152
FRAMES = 32
SLOT = 8
WIDE = FRAMES * SLOT
PARTS = ((0, 256), (256, 256), (512, 64))
CHUNKS = len(PARTS)
LAST = PARTS[2][1]
SCALE = (D ** -0.5) * 1.4426950408889634


def dot(a, b):
    return jnp.dot(a, b, preferred_element_type=F32)


def dot_nt(a, b):
    return lax.dot_general(a, b, (((1,), (1,)), ((), ())), preferred_element_type=F32)


def dot_tn(a, b):
    return lax.dot_general(a, b, (((0,), (0,)), ((), ())), preferred_element_type=F32)


def layer_norm(values, gain):
    mean = jnp.mean(values, axis=-1, keepdims=True)
    centred = values - mean
    spread = jnp.mean(centred * centred, axis=-1, keepdims=True)
    return centred * lax.rsqrt(spread + 1e-05) * gain


def kernel(
    frames, refs, norm_conv, conv_w, norm_attn, sqkv, sout, time_w, norm_time, tqkv, tout,
    out,
    xin, wc, wsq, wso,
    rims, rimr, grid, mid,
    rblk, allx, wqt, wvt, wkp, qt, kk, vt, acc, mx, al, s0, s1,
    part, psend, precv,
    asend, arecv, brecv, tgrid, tatt, oblk,
    lsem, hs, hr, cs, cr, p1s, p1r, p2s, p2r, xs, xr, ps, pr, a_s, a_r, b_s, b_r,
):
    f = lax.axis_index("frame")
    s = lax.axis_index("sp")
    x = f // 8
    y = f % 4
    z = (s // 2) * 2 + (f // 4) % 2
    core = s % 2
    zc = z * 2 + core

    def dev(px, py, pz, pc):
        px, py, pz = lax.rem(px, 4), lax.rem(py, 4), lax.rem(pz, 4)
        return ((px * 2 + pz % 2) * 4 + py, (pz // 2) * 2 + pc)

    sib = (f, (s // 2) * 2 + 1 - core)
    far = (f, lax.rem(s + 2, 4))

    loads = [
        (frames, xin),
        (refs, rblk.at[zc]),
        (sqkv, wsq),
    ]
    loads += [(conv_w.at[a, b], wc.at[b, pl.ds(a * C, C)]) for b in range(3) for a in range(3)]
    loads += [(sout, wso)]
    loads += [(time_w.at[a], wc.at[0, pl.ds(a * C, C)]) for a in range(3)]
    loads += [(tqkv.at[a], wc.at[1, pl.ds(a * C, C)]) for a in range(3)]
    loads += [(tout, wc.at[2, pl.ds(0, C)])]
    local = [pltpu.make_async_copy(a, b, lsem.at[i]) for i, (a, b) in enumerate(loads)]
    for cp in local[:13]:
        cp.start()

    bar = pltpu.get_barrier_semaphore()
    column = [(dz, dc) for dz in range(4) for dc in range(2) if dz + dc > 0]

    def col_dev(dz, dc):
        return dev(x, y, z + dz, lax.rem(core + dc, 2))

    others = [(dz, dc) for dz, dc in column if not (dz == 0 and dc == 0)]
    for dz, dc in others:
        pl.semaphore_signal(bar, inc=1, device_id=col_dev(dz, dc), device_id_type=MESH)

    for i in (1, 2, 3):
        pl.semaphore_signal(bar, inc=1, device_id=dev(x + i, y, z, core), device_id_type=MESH)
        pl.semaphore_signal(bar, inc=1, device_id=dev(x, y + i, z, core), device_id_type=MESH)

    local[0].wait()
    rim_row = lax.broadcasted_iota(jnp.int32, (96, CELLS), 0)
    rim_cell = lax.broadcasted_iota(jnp.int32, (96, CELLS), 1)
    rim = jnp.where(
        rim_cell == jnp.where(rim_row < 48, rim_row * ROWS, (rim_row - 48) * ROWS + ROWS - 1), 1.0, 0.0
    ).astype(BF)
    rims[...] = dot(rim, xin[...]).astype(BF)

    local[2].wait()
    pick = (
        lax.broadcasted_iota(jnp.int32, (OWN, C), 1)
        == lax.broadcasted_iota(jnp.int32, (OWN, C), 0) + OWN * core
    ).astype(F32).astype(BF)
    wqt[...] = dot_nt(pick, wsq[0]).astype(BF)
    wvt[...] = dot_nt(pick, wsq[2]).astype(BF)
    lane = lax.broadcasted_iota(jnp.int32, (C, MINE * 128), 1)
    row = lax.broadcasted_iota(jnp.int32, (C, MINE * 128), 0)
    spread = jnp.where(
        jnp.logical_and(lane % 128 < D, row == OWN * core + (lane // 128) * D + lane % 128), 1.0, 0.0
    ).astype(BF)
    wkp[...] = dot(wsq[1], spread).astype(BF)
    vt[:, D:, :] = jnp.where(
        lax.broadcasted_iota(jnp.int32, (MINE, 16, CHIP), 1) == 0, 1.0, 0.0
    ).astype(BF)

    def remote(src, dst, send, recv, to):
        return pltpu.make_async_remote_copy(
            src_ref=src, dst_ref=dst, send_sem=send, recv_sem=recv, device_id=to, device_id_type=MESH
        )

    gain_conv = norm_conv[...].reshape(1, C)

    def activated(v):
        v = layer_norm(v.astype(F32), gain_conv)
        return v / (1.0 + jnp.exp(-v))

    nothing = jnp.zeros((8, C), F32)

    def activate(k, _):
        v = activated(xin[pl.ds(pl.multiple_of(64 * k, 16), 64), :])
        for i in range(4):
            at = pl.multiple_of(128 * k + 32 * i, 8)
            part[pl.ds(at, 8), :] = nothing
            part[pl.ds(at + 8, ROWS), :] = v[ROWS * i : ROWS * (i + 1)]
            part[pl.ds(at + 24, 8), :] = nothing
        return 0

    lax.fori_loop(0, CELLS // 64, activate, 0)

    grid[:ROWS, :] = jnp.zeros((ROWS, 3 * C), BF)
    grid[CELLS + ROWS :, :] = jnp.zeros((ROWS, 3 * C), BF)
    for k in range(W):
        for a in range(3):
            grid[ROWS * (k + 1) : ROWS * (k + 2), a * C : (a + 1) * C] = part[
                32 * k + 7 + a : 32 * k + 7 + a + ROWS, :
            ].astype(BF)
    for i in range(3, 12):
        local[i].wait()

    def conv_tap(b):
        return dot(grid[ROWS * b : ROWS * b + CELLS, :], wc[b])

    pl.semaphore_wait(bar, 13)
    up = remote(
        rims.at[pl.ds(0, 48)], rimr.at[pl.ds(48, 48)], hs.at[0], hr.at[0], (f, jnp.maximum(s - 1, 0))
    )
    down = remote(
        rims.at[pl.ds(48, 48)], rimr.at[pl.ds(0, 48)], hs.at[1], hr.at[1], (f, jnp.minimum(s + 1, 3))
    )

    @pl.when(s > 0)
    def _():
        up.start()

    @pl.when(s < 3)
    def _():
        down.start()

    col = [
        remote(rblk.at[zc], rblk.at[zc], cs.at[i], cr.at[i], col_dev(dz, dc))
        for i, (dz, dc) in enumerate(column)
    ]
    local[1].wait()
    for cp in col:
        cp.start()


    mid[...] = conv_tap(0)
    mid[...] += conv_tap(1)
    mid[...] += conv_tap(2)

    def patch(tap, first, values):
        rim = activated(values).astype(BF)
        for b in range(3):
            part[64 * b : 64 * b + 8, :] = nothing
            part[64 * b + 8 : 64 * b + 56, :] = dot(rim, wc[b, tap * C : (tap + 1) * C, :])
        part[192 : 192 + W, :] = part[7 : 7 + W, :] + part[72 : 72 + W, :] + part[137 : 137 + W, :]
        for k in range(W):
            mid[ROWS * k + first : ROWS * k + first + 1, :] += part[192 + k : 193 + k, :]

    @pl.when(s > 0)
    def _():
        down.wait_recv()
        patch(0, 0, rimr[:48])

    @pl.when(s < 3)
    def _():
        up.wait_recv()
        patch(2, ROWS - 1, rimr[48:])

    @pl.when(s > 0)
    def _():
        up.wait_send()

    @pl.when(s < 3)
    def _():
        down.wait_send()

    for cp in local[13:]:
        cp.start()
    gain_attn = norm_attn[...].reshape(1, C)

    def settle(k, _):
        at = pl.ds(pl.multiple_of(144 * k, 16), 144)
        middle = (xin[at, :].astype(F32) + mid[at, :]).astype(BF).astype(F32)
        mid[at, :] = middle
        allx[0, 0, k] = layer_norm(middle, gain_attn).astype(BF)
        return 0

    lax.fori_loop(0, 4, settle, 0)

    to_sib = remote(allx.at[0, 0], allx.at[0, 1], xs.at[0], xr.at[0], sib)
    to_far = remote(allx.at[0, 0], allx.at[3, 0], xs.at[1], xr.at[1], far)
    to_far.start()
    for cp in col:
        cp.wait()
    for i in range(8):
        tatt[pl.ds(18 * i, 18), :] = rblk[i].astype(F32)
    mine = jnp.int32(1) + x // 2
    allx[mine, lax.rem(x, 2), y] = tatt[:144, :].astype(BF)


    def share(first, count):
        return pl.ds(pl.multiple_of(first, 16), count)

    half = share(64 * core, 80)

    def line_one(i):
        return dev(x + i * (1 - core), y + i * core, z, core)

    def line_two(i):
        return dev(x + i * core, y + i * (1 - core), z, core)

    def home(i):
        px, py = lax.rem(x + 4 - i * (1 - core), 4), lax.rem(y + 4 - i * core, 4)
        return allx.at[1 + px // 2, lax.rem(px, 2), py, half]

    p1 = [remote(home(0), home(0), p1s.at[i - 1], p1r.at[i - 1], line_one(i)) for i in (1, 2, 3)]
    p2 = [
        [
            remote(home(k), home(k), p2s.at[k, i - 1], p2r.at[k, i - 1], line_two(i))
            for i in (1, 2, 3)
        ]
        for k in range(4)
    ]
    for cp in p1 + p2[0]:
        cp.start()
    to_sib.start()

    relay = remote(allx.at[3, 0], allx.at[3, 1], xs.at[2], xr.at[2], sib)
    ref_swap = [
        remote(
            allx.at[k, :, :, share(80 * core, 64)], allx.at[k, :, :, share(80 * core, 64)],
            xs.at[2 + k], xr.at[2 + k], sib,
        )
        for k in (1, 2)
    ]

    acc[...] = jnp.zeros_like(acc)
    mx[...] = jnp.full_like(mx, -1e30)
    to_sib.wait_recv()
    own, next_door = allx[0, 0].reshape(CELLS, C), allx[0, 1].reshape(CELLS, C)
    asking = jnp.concatenate(
        [cells[lo : lo + n] for lo, n in PARTS for cells in (own, next_door)], axis=0
    )
    qall = dot_nt(wqt[...], asking) * SCALE
    qt[...] = qall.astype(BF)
    for i in range(3):
        p1[i].wait()
        for cp in p2[i + 1]:
            cp.start()

    def scores(h, sref, lo=0, n=CHIP):
        at = slice(lo, lo + n)
        sc = dot(kk[h][:, :D], qt[h * D : (h + 1) * D, at])
        sref[:, :n] = sc
        old = mx[h, :, at]
        new = jnp.maximum(old, jnp.max(sc, axis=0, keepdims=True))
        mx[h, :, at] = new
        al[h, :, at] = jnp.exp2(old - new)

    def weigh(h, sref, lo=0, n=CHIP):
        at = slice(lo, lo + n)
        p = jnp.exp2(sref[:, :n] - mx[h, :, at]).astype(BF)
        acc[h, :, at] = acc[h, :, at] * al[h, :, at] + dot(vt[h], p)

    def project(c):
        rows = allx[c].reshape(CHIP, C)
        keys = dot(rows, wkp[...])
        vals = dot_nt(wvt[...], rows)
        for h in range(MINE):
            kk[h] = keys[:, h * 128 : (h + 1) * 128].astype(BF)
            vt[h, :D, :] = vals[h * D : (h + 1) * D, :].astype(BF)

    def attend(c, _):
        @pl.when(c == 1)
        def _():
            ref_swap[0].wait_recv()

        @pl.when(c == 2)
        def _():
            ref_swap[1].wait_recv()
            to_far.wait_recv()
            relay.start()

        project(c)
        scores(0, s0)
        weigh(0, s0)
        scores(1, s1)
        weigh(1, s1)
        scores(2, s0)

        weigh(2, s0)
        scores(3, s1)
        weigh(3, s1)

        @pl.when(c == 0)
        def _():
            for line in p2:
                for cp in line:
                    cp.wait()
            for cp in ref_swap:
                cp.start()

        return 0

    lax.fori_loop(0, 3, attend, 0)
    relay.wait_recv()
    project(3)
    local[12].wait()
    wout = wso[pl.ds(pl.multiple_of(OWN * core, 16), OWN), :]
    swaps = [
        remote(psend.at[pl.ds(lo, n)], precv.at[pl.ds(lo, n)], ps.at[j], pr.at[j], sib)
        for j, (lo, n) in enumerate(PARTS)
    ]
    wide_row = lax.broadcasted_iota(jnp.int32, (WIDE, LAST), 0)
    last_row = lax.broadcasted_iota(jnp.int32, (WIDE, LAST), 1)
    few = LAST // FRAMES
    fan = jnp.where(
        jnp.logical_and(wide_row % SLOT < few, last_row == (wide_row // SLOT) * few + wide_row % SLOT),
        1.0, 0.0,
    ).astype(BF)

    def to_all(src, dst, send, recv, j):
        def go(i, _):
            peer = lax.rem(f + i, FRAMES)
            remote(src.at[j, peer], dst.at[j, f], send.at[j], recv.at[j], (peer, s)).start()
            return 0

        lax.fori_loop(1, FRAMES, go, 0)
        dst[j, f] = src[j, f]

    def from_all(src, dst, send, recv, j):
        every = pl.ds(0, FRAMES - 1)
        remote(src.at[j, every], dst.at[j, every], send.at[j], recv.at[j], sib).wait()

    def out_project(j):
        lo, n = PARTS[j]
        at = slice(2 * lo, 2 * lo + 2 * n)
        for h in range(MINE):
            qt[h * D : (h + 1) * D, at] = (acc[h, :D, at] / acc[h, D : D + 1, at]).astype(BF)
        part[at, :] = dot_tn(qt[:, at], wout)
        psend[lo : lo + n, :] = part[2 * lo + n : 2 * lo + 2 * n, :].astype(BF)
        swaps[j].start()

    def depart(j):
        lo, n = PARTS[j]
        swaps[j].wait()
        at = slice(lo, lo + n)
        after = mid[at, :] + part[2 * lo : 2 * lo + n, :] + precv[at, :].astype(F32)
        if n < WIDE:
            after = dot(fan, after.astype(BF))
        asend[j] = after.reshape(FRAMES, SLOT, C).astype(BF)
        to_all(asend, arecv, a_s, a_r, j)

    items = [(j, h) for j in range(CHUNKS) for h in range(MINE)]

    def span(j):
        return 2 * PARTS[j][0], 2 * PARTS[j][1]

    scores(0, s0, *span(0))
    for i, (j, h) in enumerate(items):
        weigh(h, (s0, s1)[i % 2], *span(j))
        if i + 1 < len(items):
            jn, hn = items[i + 1]
            scores(hn, (s0, s1)[(i + 1) % 2], *span(jn))
        if h == MINE - 1:
            out_project(j)
        if j > 0 and h == 1:
            depart(j - 1)
    for i in range(13, len(local)):
        local[i].wait()
    depart(CHUNKS - 1)

    to_sib.wait_send()
    to_far.wait_send()
    relay.wait_send()
    for cp in ref_swap:
        cp.wait_send()

    gain_time = norm_time[...].reshape(1, C)
    zero = jnp.zeros((SLOT, C), F32)
    same = (
        lax.broadcasted_iota(jnp.int32, (WIDE, WIDE), 0) % SLOT
        == lax.broadcasted_iota(jnp.int32, (WIDE, WIDE), 1) % SLOT
    )
    def through_time(j, _):
        from_all(asend, arecv, a_s, a_r, j)
        block = arecv[j].astype(F32).reshape(WIDE, C)
        tgrid[:, :C] = jnp.concatenate([zero, block[:-SLOT]], axis=0).astype(BF)
        tgrid[:, C : 2 * C] = block.astype(BF)
        tgrid[:, 2 * C :] = jnp.concatenate([block[SLOT:], zero], axis=0).astype(BF)
        timed = (block + dot(tgrid[...], wc[0])).astype(BF).astype(F32)
        tn = layer_norm(timed, gain_time).astype(BF)
        q = (dot(tn, wc[1, 0 * C : 1 * C, :]) * SCALE).astype(BF)
        k = dot(tn, wc[1, 1 * C : 2 * C, :]).astype(BF)
        v = dot(tn, wc[1, 2 * C : 3 * C, :]).astype(BF)
        for h in range(HEADS):
            lo, hi = (h * D) // 128 * 128, -(-((h + 1) * D) // 128) * 128
            ln = lax.broadcasted_iota(jnp.int32, (1, hi - lo), 1) + lo
            inside = jnp.logical_and(ln >= h * D, ln < (h + 1) * D)
            qh = q[:, lo:hi] * jnp.where(inside, 1.0, 0.0).astype(BF)
            sc = jnp.where(same, dot_nt(qh, k[:, lo:hi]), -1e30)
            e = jnp.exp2(sc - jnp.max(sc, axis=1, keepdims=True))
            total = jnp.sum(e, axis=1, keepdims=True)
            o = dot(e.astype(BF), v[:, lo:hi]) / total
            if h == 0:
                tatt[:, lo:hi] = o
            else:
                tatt[:, lo:hi] = jnp.where(inside, o, tatt[:, lo:hi])
        res = timed + dot(tatt[...].astype(BF), wc[2, :C, :])
        asend[j] = res.reshape(FRAMES, SLOT, C).astype(BF)
        to_all(asend, brecv, b_s, b_r, j)
        return 0

    lax.fori_loop(0, CHUNKS, through_time, 0)

    for j, (lo, n) in enumerate(PARTS):
        from_all(asend, brecv, b_s, b_r, j)
        got = brecv[j].astype(F32).reshape(WIDE, C)
        if n < WIDE:
            got = dot_tn(fan, got.astype(BF))
        oblk[lo : lo + n, :] = got.astype(BF)
    done = pltpu.make_async_copy(oblk, out, lsem.at[0])
    done.start()
    done.wait()


def block(
    frames_in, reference_rows, norm_conv, conv_weight, norm_attn, spatial_qkv, spatial_out,
    time_weight, norm_time, temporal_qkv, temporal_out,
):
    hbm = pl.BlockSpec(memory_space=pl.ANY)
    vm = pl.BlockSpec(memory_space=pltpu.VMEM)
    v = pltpu.VMEM
    dma = pltpu.SemaphoreType.DMA
    scratch = [
        v((CELLS, C), BF), v((3, 3 * C, C), BF), v((3, C, C), BF), v((C, C), BF),
        v((96, C), BF), v((96, C), BF), v((CELLS + 2 * ROWS, 3 * C), BF), v((CELLS, C), F32),
        v((8, 18, C), BF), v((4, 2, 4, 144, C), BF), v((OWN, C), BF), v((OWN, C), BF),
        v((C, MINE * 128), BF), v((OWN, CHIP), BF), v((MINE, CHIP, 128), BF), v((MINE, 96, CHIP), BF),
        v((MINE, 96, CHIP), F32), v((MINE, 1, CHIP), F32), v((MINE, 1, CHIP), F32),
        v((CHIP, CHIP), F32), v((CHIP, CHIP), F32),
        v((CHIP, C), F32), v((CELLS, C), BF), v((CELLS, C), BF),
        v((CHUNKS, FRAMES, SLOT, C), BF), v((CHUNKS, FRAMES, SLOT, C), BF),
        v((CHUNKS, FRAMES, SLOT, C), BF),
        v((WIDE, 3 * C), BF), v((WIDE, C), F32), v((CELLS, C), BF),
        dma((20,)), dma((2,)), dma((2,)), dma((7,)), dma((7,)),
        dma((3,)), dma((3,)), dma((4, 3)), dma((4, 3)), dma((5,)), dma((5,)), dma((3,)), dma((3,)),
        dma((CHUNKS,)), dma((CHUNKS,)), dma((CHUNKS,)), dma((CHUNKS,)),
    ]
    cells = frames_in.transpose(0, 2, 1, 3).reshape(CELLS, C)
    res = pl.pallas_call(
        kernel,
        out_shape=jax.ShapeDtypeStruct((CELLS, C), BF),
        in_specs=[hbm, hbm, vm, hbm, vm, hbm, hbm, hbm, vm, hbm, hbm],
        out_specs=hbm,
        scratch_shapes=scratch,
        compiler_params=pltpu.CompilerParams(
            collective_id=0, has_side_effects=True, vmem_limit_bytes=62 * 2**20
        ),
    )(
        cells, reference_rows, norm_conv, conv_weight, norm_attn, spatial_qkv, spatial_out,
        time_weight, norm_time, temporal_qkv, temporal_out,
    )
    return res.reshape(1, W, ROWS, C).transpose(0, 2, 1, 3)


def solution(mesh):
    rep = P()
    in_specs = (P("frame", "sp", None, None), P(("frame", "sp"), None)) + (rep,) * 9
    return jax.shard_map(
        block, mesh=mesh, in_specs=in_specs, out_specs=P("frame", "sp", None, None), check_vma=False
    )
```

time: 106 us -> 90.5 us (0.85)
  Pallas kernels: 96.6 us -> 87.4 us
  local copies, waits for them, and re-layouts: 8.05 us -> 2.04 us
    pallas_call x1, Pallas kernels: 96.6 us -> 87.4 us  [block(): pl.pallas_call(kernel, out_shape=jax.ShapeDtypeStruct((CELLS, C), BF), in...]
    reshape x3 -> x0, local copies, waits for them, and re-layouts: 3.82 us -> none  [the longest x1 1.28 us: block(): norm_time.reshape(1, C)]
    pallas_call x1 -> x0, local copies, waits for them, and re-layouts: 2.09 us -> none  [block(): pl.pallas_call(kernel, out_shape=jax.ShapeDtypeStruct(frames_in.shape, BF...]
where the time goes in v1:
time: 90.5 us; the launch traced here: 89.5 us
  Pallas kernels  87.4 us (97%)
  local copies, waits for them, and re-layouts  2.04 us (2%)
    pallas_call x1, Pallas kernels, block(): pl.pallas_call(kernel, out_shape=jax.ShapeDtypeStruct((CELLS, C), BF), in...  87.4 us
    unnamed x1, local copies, waits for them, and re-layouts  2.04 us

profile of v1, /device:TPU:1, one launch (start us, length us, event | category | flops | bytes accessed | tf_op | source)
XLA Modules:
  0.0 89.5 jit_solution(9334228635333955172)
XLA Ops:
  0.0 87.4 %shard_map.109 = bf16[576,640]{1,0:T(8,128)(2,1)} custom-call(bf16[576,640]{1,0:T(8,128)(2,1)} %bitcast.7, bf16[18,640]{1,0:T(8,128)(2,1)} %refs.1, f32[640]{0:T(1024)} %norm_conv.1, bf16[3,3,640,640]{3,2,1,0:T(8,128)(2,1)} %conv_w.1, f32[640]{0:T(1024)} %norm_attn.1, bf16[3,640,640]{2,1,0:T(8,128)(2,1)} %sqkv.1, bf16[640,640]{1,0:T(8,128)(2,1)} %sout.1, ...), custom_call_target="tpu_custom_call" | custom-call | tf_op jit(solution)/shard_map/pallas_call | solution.py:495
  87.4 2.0 %copy.13 = bf16[1,16,36,640]{3,1,2,0:T(8,128)(2,1)} copy(bf16[1,16,36,640]{3,1,2,0:T(8,128)(2,1)} %bitcast.6) | data formatting | bytes 1474560

commit v2 on v1

--- a/solution.py
+++ b/solution.py
@@ -191,6 +191,40 @@
     mid[...] += conv_tap(1)
     mid[...] += conv_tap(2)
 
+    for cp in col:
+        cp.wait()
+    for i in range(8):
+        tatt[pl.ds(18 * i, 18), :] = rblk[i].astype(F32)
+    mine = jnp.int32(1) + x // 2
+    allx[mine, lax.rem(x, 2), y] = tatt[:144, :].astype(BF)
+
+
+    def share(first, count):
+        return pl.ds(pl.multiple_of(first, 16), count)
+
+    half = share(64 * core, 80)
+
+    def line_one(i):
+        return dev(x + i * (1 - core), y + i * core, z, core)
+
+    def line_two(i):
+        return dev(x + i * core, y + i * (1 - core), z, core)
+
+    def home(i):
+        px, py = lax.rem(x + 4 - i * (1 - core), 4), lax.rem(y + 4 - i * core, 4)
+        return allx.at[1 + px // 2, lax.rem(px, 2), py, half]
+
+    p1 = [remote(home(0), home(0), p1s.at[i - 1], p1r.at[i - 1], line_one(i)) for i in (1, 2, 3)]
+    p2 = [
+        [
+            remote(home(k), home(k), p2s.at[k, i - 1], p2r.at[k, i - 1], line_two(i))
+            for i in (1, 2, 3)
+        ]
+        for k in range(4)
+    ]
+    for cp in p1 + p2[0]:
+        cp.start()
+
     def patch(tap, first, values):
         rim = activated(values).astype(BF)
         for b in range(3):
@@ -234,41 +268,7 @@
     to_sib = remote(allx.at[0, 0], allx.at[0, 1], xs.at[0], xr.at[0], sib)
     to_far = remote(allx.at[0, 0], allx.at[3, 0], xs.at[1], xr.at[1], far)
     to_far.start()
-    for cp in col:
-        cp.wait()
-    for i in range(8):
-        tatt[pl.ds(18 * i, 18), :] = rblk[i].astype(F32)
-    mine = jnp.int32(1) + x // 2
-    allx[mine, lax.rem(x, 2), y] = tatt[:144, :].astype(BF)
-
-
-    def share(first, count):
-        return pl.ds(pl.multiple_of(first, 16), count)
-
-    half = share(64 * core, 80)
-
-    def line_one(i):
-        return dev(x + i * (1 - core), y + i * core, z, core)
-
-    def line_two(i):
-        return dev(x + i * core, y + i * (1 - core), z, core)
-
-    def home(i):
-        px, py = lax.rem(x + 4 - i * (1 - core), 4), lax.rem(y + 4 - i * core, 4)
-        return allx.at[1 + px // 2, lax.rem(px, 2), py, half]
-
-    p1 = [remote(home(0), home(0), p1s.at[i - 1], p1r.at[i - 1], line_one(i)) for i in (1, 2, 3)]
-    p2 = [
-        [
-            remote(home(k), home(k), p2s.at[k, i - 1], p2r.at[k, i - 1], line_two(i))
-            for i in (1, 2, 3)
-        ]
-        for k in range(4)
-    ]
-    for cp in p1 + p2[0]:
-        cp.start()
     to_sib.start()
-
     relay = remote(allx.at[3, 0], allx.at[3, 1], xs.at[2], xr.at[2], sib)
     ref_swap = [
         remote(
@@ -363,13 +363,16 @@
         1.0, 0.0,
     ).astype(BF)
 
+    hops = sorted(
+        ((dx, dz, dy) for dx in range(4) for dz in range(2) for dy in range(4) if dx + dz + dy),
+        key=lambda d: -(min(d[0], 4 - d[0]) + d[1] + min(d[2], 4 - d[2])),
+    )
+    zl = (f // 4) % 2
+    rounds = [lax.rem(x + dx, 4) * 8 + lax.rem(zl + dz, 2) * 4 + lax.rem(y + dy, 4) for dx, dz, dy in hops]
+
     def to_all(src, dst, send, recv, j):
-        def go(i, _):
-            peer = lax.rem(f + i, FRAMES)
+        for peer in rounds:
             remote(src.at[j, peer], dst.at[j, f], send.at[j], recv.at[j], (peer, s)).start()
-            return 0
-
-        lax.fori_loop(1, FRAMES, go, 0)
         dst[j, f] = src[j, f]
 
     def from_all(src, dst, send, recv, j):
@@ -422,17 +425,14 @@
 
     gain_time = norm_time[...].reshape(1, C)
     zero = jnp.zeros((SLOT, C), F32)
-    same = (
-        lax.broadcasted_iota(jnp.int32, (WIDE, WIDE), 0) % SLOT
-        == lax.broadcasted_iota(jnp.int32, (WIDE, WIDE), 1) % SLOT
-    )
-    def through_time(j, _):
-        from_all(asend, arecv, a_s, a_r, j)
-        block = arecv[j].astype(F32).reshape(WIDE, C)
-        tgrid[:, :C] = jnp.concatenate([zero, block[:-SLOT]], axis=0).astype(BF)
-        tgrid[:, C : 2 * C] = block.astype(BF)
-        tgrid[:, 2 * C :] = jnp.concatenate([block[SLOT:], zero], axis=0).astype(BF)
-        timed = (block + dot(tgrid[...], wc[0])).astype(BF).astype(F32)
+    def same_cell(n, cells):
+        return (
+            lax.broadcasted_iota(jnp.int32, (n, n), 0) % cells
+            == lax.broadcasted_iota(jnp.int32, (n, n), 1) % cells
+        )
+
+    def through_time(block, n, same):
+        timed = (block + dot(tgrid[:n, :], wc[0])).astype(BF).astype(F32)
         tn = layer_norm(timed, gain_time).astype(BF)
         q = (dot(tn, wc[1, 0 * C : 1 * C, :]) * SCALE).astype(BF)
         k = dot(tn, wc[1, 1 * C : 2 * C, :]).astype(BF)
@@ -447,25 +447,59 @@
             total = jnp.sum(e, axis=1, keepdims=True)
             o = dot(e.astype(BF), v[:, lo:hi]) / total
             if h == 0:
-                tatt[:, lo:hi] = o
+                tatt[:n, lo:hi] = o
             else:
-                tatt[:, lo:hi] = jnp.where(inside, o, tatt[:, lo:hi])
-        res = timed + dot(tatt[...].astype(BF), wc[2, :C, :])
+                tatt[:n, lo:hi] = jnp.where(inside, o, tatt[:n, lo:hi])
+        return timed + dot(tatt[:n, :].astype(BF), wc[2, :C, :])
+
+    all_rows = same_cell(WIDE, SLOT)
+
+    def full_part(j, _):
+        from_all(asend, arecv, a_s, a_r, j)
+        block = arecv[j].astype(F32).reshape(WIDE, C)
+        tgrid[:, :C] = jnp.concatenate([zero, block[:-SLOT]], axis=0).astype(BF)
+        tgrid[:, C : 2 * C] = block.astype(BF)
+        tgrid[:, 2 * C :] = jnp.concatenate([block[SLOT:], zero], axis=0).astype(BF)
+        res = through_time(block, WIDE, all_rows)
         asend[j] = res.reshape(FRAMES, SLOT, C).astype(BF)
         to_all(asend, brecv, b_s, b_r, j)
         return 0
 
-    lax.fori_loop(0, CHUNKS, through_time, 0)
-
+    lax.fori_loop(0, CHUNKS - 1, full_part, 0)
+
+    last = CHUNKS - 1
+    at_row = lax.broadcasted_iota(jnp.int32, (LAST, WIDE), 0)
+    from_row = lax.broadcasted_iota(jnp.int32, (LAST, WIDE), 1)
+    from_all(asend, arecv, a_s, a_r, last)
+    wide = arecv[last].astype(F32).reshape(WIDE, C).astype(BF)
+    drawn = [
+        dot(
+            jnp.where(
+                from_row == (at_row // few + t - 1) * SLOT + at_row % few, 1.0, 0.0
+            ).astype(BF),
+            wide,
+        )
+        for t in range(3)
+    ]
+    for t in range(3):
+        tgrid[:LAST, t * C : (t + 1) * C] = drawn[t].astype(BF)
+    res = through_time(drawn[1], LAST, same_cell(LAST, few))
+    asend[last] = dot(fan, res.astype(BF)).reshape(FRAMES, SLOT, C).astype(BF)
+    to_all(asend, brecv, b_s, b_r, last)
+
+    done = [
+        pltpu.make_async_copy(oblk.at[pl.ds(lo, n)], out.at[pl.ds(lo, n)], lsem.at[j])
+        for j, (lo, n) in enumerate(PARTS)
+    ]
     for j, (lo, n) in enumerate(PARTS):
         from_all(asend, brecv, b_s, b_r, j)
         got = brecv[j].astype(F32).reshape(WIDE, C)
         if n < WIDE:
             got = dot_tn(fan, got.astype(BF))
         oblk[lo : lo + n, :] = got.astype(BF)
-    done = pltpu.make_async_copy(oblk, out, lsem.at[0])
-    done.start()
-    done.wait()
+        done[j].start()
+    for cp in done:
+        cp.wait()
 
 
 def block(

time: 90.5 us -> 88 us (0.972)
  Pallas kernels: 87.4 us -> 85.8 us
    pallas_call x1, Pallas kernels: 87.4 us -> 85.8 us  [block(): pl.pallas_call(kernel, out_shape=jax.ShapeDtypeStruct((CELLS, C), BF), in...]
where the time goes in v2:
time: 88 us; the launch traced here: 87.8 us
  Pallas kernels  85.8 us (98%)
  local copies, waits for them, and re-layouts  2.04 us (2%)
    pallas_call x1, Pallas kernels, block(): pl.pallas_call(kernel, out_shape=jax.ShapeDtypeStruct((CELLS, C), BF), in...  85.8 us
    unnamed x1, local copies, waits for them, and re-layouts  2.04 us

profile of v2, /device:TPU:1, one launch (start us, length us, event | category | flops | bytes accessed | tf_op | source)
XLA Modules:
  0.0 87.8 jit_solution(1336784839192918603)
XLA Ops:
  0.0 85.8 %shard_map.109 = bf16[576,640]{1,0:T(8,128)(2,1)} custom-call(bf16[576,640]{1,0:T(8,128)(2,1)} %bitcast.7, bf16[18,640]{1,0:T(8,128)(2,1)} %refs.1, f32[640]{0:T(1024)} %norm_conv.1, bf16[3,3,640,640]{3,2,1,0:T(8,128)(2,1)} %conv_w.1, f32[640]{0:T(1024)} %norm_attn.1, bf16[3,640,640]{2,1,0:T(8,128)(2,1)} %sqkv.1, bf16[640,640]{1,0:T(8,128)(2,1)} %sout.1, ...), custom_call_target="tpu_custom_call" | custom-call | tf_op jit(solution)/shard_map/pallas_call | solution.py:529
  85.8 2.0 %copy.13 = bf16[1,16,36,640]{3,1,2,0:T(8,128)(2,1)} copy(bf16[1,16,36,640]{3,1,2,0:T(8,128)(2,1)} %bitcast.6) | data formatting | bytes 1474560

commit v3 on v2

--- a/solution.py
+++ b/solution.py
@@ -54,7 +54,7 @@
     rims, rimr, grid, mid,
     rblk, allx, wqt, wvt, wkp, qt, kk, vt, acc, mx, al, s0, s1,
     part, psend, precv,
-    asend, arecv, brecv, tgrid, tatt, oblk,
+    asend, arecv, brecv, lsend, lrecv, lback, tgrid, tatt, oblk,
     lsem, hs, hr, cs, cr, p1s, p1r, p2s, p2r, xs, xr, ps, pr, a_s, a_r, b_s, b_r,
 ):
     f = lax.axis_index("frame")
@@ -355,13 +355,37 @@
         remote(psend.at[pl.ds(lo, n)], precv.at[pl.ds(lo, n)], ps.at[j], pr.at[j], sib)
         for j, (lo, n) in enumerate(PARTS)
     ]
-    wide_row = lax.broadcasted_iota(jnp.int32, (WIDE, LAST), 0)
-    last_row = lax.broadcasted_iota(jnp.int32, (WIDE, LAST), 1)
     few = LAST // FRAMES
-    fan = jnp.where(
-        jnp.logical_and(wide_row % SLOT < few, last_row == (wide_row // SLOT) * few + wide_row % SLOT),
-        1.0, 0.0,
-    ).astype(BF)
+    tall = FRAMES * 16
+
+    def pack(values):
+        slot_row = lax.broadcasted_iota(jnp.int32, (tall, LAST), 0)
+        cell = lax.broadcasted_iota(jnp.int32, (tall, LAST), 1)
+        total = None
+        for t in range(C // 128):
+            want = slot_row - t * few
+            hit = jnp.logical_and(want % 16 < few, cell == (slot_row // 16) * few + want % 16)
+            hit = jnp.logical_and(hit, want % 16 == slot_row % 16 - t * few)
+            term = dot(jnp.where(hit, 1.0, 0.0).astype(BF), values[:, 128 * t : 128 * (t + 1)])
+            total = term if total is None else total + term
+        return total.reshape(FRAMES, 16, 128).astype(BF)
+
+    def unpack(slots):
+        slot_row = lax.broadcasted_iota(jnp.int32, (LAST, tall), 1)
+        cell = lax.broadcasted_iota(jnp.int32, (LAST, tall), 0)
+        flat = slots.reshape(tall, 128)
+        return jnp.concatenate(
+            [
+                dot(
+                    jnp.where(
+                        slot_row == (cell // few) * 16 + t * few + cell % few, 1.0, 0.0
+                    ).astype(BF),
+                    flat,
+                )
+                for t in range(C // 128)
+            ],
+            axis=1,
+        )
 
     hops = sorted(
         ((dx, dz, dy) for dx in range(4) for dz in range(2) for dy in range(4) if dx + dz + dy),
@@ -370,14 +394,14 @@
     zl = (f // 4) % 2
     rounds = [lax.rem(x + dx, 4) * 8 + lax.rem(zl + dz, 2) * 4 + lax.rem(y + dy, 4) for dx, dz, dy in hops]
 
-    def to_all(src, dst, send, recv, j):
+    def to_all(src, dst, send, recv):
         for peer in rounds:
-            remote(src.at[j, peer], dst.at[j, f], send.at[j], recv.at[j], (peer, s)).start()
-        dst[j, f] = src[j, f]
-
-    def from_all(src, dst, send, recv, j):
+            remote(src.at[peer], dst.at[f], send, recv, (peer, s)).start()
+        dst[f] = src[f]
+
+    def from_all(src, dst, send, recv):
         every = pl.ds(0, FRAMES - 1)
-        remote(src.at[j, every], dst.at[j, every], send.at[j], recv.at[j], sib).wait()
+        remote(src.at[every], dst.at[every], send, recv, sib).wait()
 
     def out_project(j):
         lo, n = PARTS[j]
@@ -394,9 +418,11 @@
         at = slice(lo, lo + n)
         after = mid[at, :] + part[2 * lo : 2 * lo + n, :] + precv[at, :].astype(F32)
         if n < WIDE:
-            after = dot(fan, after.astype(BF))
-        asend[j] = after.reshape(FRAMES, SLOT, C).astype(BF)
-        to_all(asend, arecv, a_s, a_r, j)
+            lsend[...] = pack(after.astype(BF))
+            to_all(lsend, lrecv, a_s.at[j], a_r.at[j])
+        else:
+            asend[j] = after.reshape(FRAMES, SLOT, C).astype(BF)
+            to_all(asend.at[j], arecv.at[j], a_s.at[j], a_r.at[j])
 
     items = [(j, h) for j in range(CHUNKS) for h in range(MINE)]
 
@@ -455,47 +481,42 @@
     all_rows = same_cell(WIDE, SLOT)
 
     def full_part(j, _):
-        from_all(asend, arecv, a_s, a_r, j)
+        from_all(asend.at[j], arecv.at[j], a_s.at[j], a_r.at[j])
         block = arecv[j].astype(F32).reshape(WIDE, C)
         tgrid[:, :C] = jnp.concatenate([zero, block[:-SLOT]], axis=0).astype(BF)
         tgrid[:, C : 2 * C] = block.astype(BF)
         tgrid[:, 2 * C :] = jnp.concatenate([block[SLOT:], zero], axis=0).astype(BF)
         res = through_time(block, WIDE, all_rows)
         asend[j] = res.reshape(FRAMES, SLOT, C).astype(BF)
-        to_all(asend, brecv, b_s, b_r, j)
+        to_all(asend.at[j], brecv.at[j], b_s.at[j], b_r.at[j])
         return 0
 
     lax.fori_loop(0, CHUNKS - 1, full_part, 0)
 
     last = CHUNKS - 1
-    at_row = lax.broadcasted_iota(jnp.int32, (LAST, WIDE), 0)
-    from_row = lax.broadcasted_iota(jnp.int32, (LAST, WIDE), 1)
-    from_all(asend, arecv, a_s, a_r, last)
-    wide = arecv[last].astype(F32).reshape(WIDE, C).astype(BF)
-    drawn = [
-        dot(
-            jnp.where(
-                from_row == (at_row // few + t - 1) * SLOT + at_row % few, 1.0, 0.0
-            ).astype(BF),
-            wide,
-        )
-        for t in range(3)
-    ]
-    for t in range(3):
-        tgrid[:LAST, t * C : (t + 1) * C] = drawn[t].astype(BF)
-    res = through_time(drawn[1], LAST, same_cell(LAST, few))
-    asend[last] = dot(fan, res.astype(BF)).reshape(FRAMES, SLOT, C).astype(BF)
-    to_all(asend, brecv, b_s, b_r, last)
+    at_row = lax.broadcasted_iota(jnp.int32, (LAST, LAST), 0)
+    from_row = lax.broadcasted_iota(jnp.int32, (LAST, LAST), 1)
+    from_all(lsend, lrecv, a_s.at[last], a_r.at[last])
+    block = unpack(lrecv[...])
+    tgrid[:LAST, C : 2 * C] = block.astype(BF)
+    for t in (0, 2):
+        near = jnp.where(from_row == at_row + (t - 1) * few, 1.0, 0.0).astype(BF)
+        tgrid[:LAST, t * C : (t + 1) * C] = dot(near, block.astype(BF)).astype(BF)
+    res = through_time(block, LAST, same_cell(LAST, few))
+    lsend[...] = pack(res.astype(BF))
+    to_all(lsend, lback, b_s.at[last], b_r.at[last])
 
     done = [
         pltpu.make_async_copy(oblk.at[pl.ds(lo, n)], out.at[pl.ds(lo, n)], lsem.at[j])
         for j, (lo, n) in enumerate(PARTS)
     ]
     for j, (lo, n) in enumerate(PARTS):
-        from_all(asend, brecv, b_s, b_r, j)
-        got = brecv[j].astype(F32).reshape(WIDE, C)
         if n < WIDE:
-            got = dot_tn(fan, got.astype(BF))
+            from_all(lsend, lback, b_s.at[j], b_r.at[j])
+            got = unpack(lback[...])
+        else:
+            from_all(asend.at[j], brecv.at[j], b_s.at[j], b_r.at[j])
+            got = brecv[j].astype(F32).reshape(WIDE, C)
         oblk[lo : lo + n, :] = got.astype(BF)
         done[j].start()
     for cp in done:
@@ -518,8 +539,9 @@
         v((MINE, 96, CHIP), F32), v((MINE, 1, CHIP), F32), v((MINE, 1, CHIP), F32),
         v((CHIP, CHIP), F32), v((CHIP, CHIP), F32),
         v((CHIP, C), F32), v((CELLS, C), BF), v((CELLS, C), BF),
-        v((CHUNKS, FRAMES, SLOT, C), BF), v((CHUNKS, FRAMES, SLOT, C), BF),
-        v((CHUNKS, FRAMES, SLOT, C), BF),
+        v((CHUNKS - 1, FRAMES, SLOT, C), BF), v((CHUNKS - 1, FRAMES, SLOT, C), BF),
+        v((CHUNKS - 1, FRAMES, SLOT, C), BF),
+        v((FRAMES, 16, 128), BF), v((FRAMES, 16, 128), BF), v((FRAMES, 16, 128), BF),
         v((WIDE, 3 * C), BF), v((WIDE, C), F32), v((CELLS, C), BF),
         dma((20,)), dma((2,)), dma((2,)), dma((7,)), dma((7,)),
         dma((3,)), dma((3,)), dma((4, 3)), dma((4, 3)), dma((5,)), dma((5,)), dma((3,)), dma((3,)),

time: 88 us -> 86 us (0.977)
  Pallas kernels: 85.8 us -> 83.8 us
    pallas_call x1, Pallas kernels: 85.8 us -> 83.8 us  [block(): pl.pallas_call(kernel, out_shape=jax.ShapeDtypeStruct((CELLS, C), BF), in...]
where the time goes in v3:
time: 86 us; the launch traced here: 85.8 us
  Pallas kernels  83.8 us (97%)
  local copies, waits for them, and re-layouts  2.04 us (2%)
    pallas_call x1, Pallas kernels, block(): pl.pallas_call(kernel, out_shape=jax.ShapeDtypeStruct((CELLS, C), BF), in...  83.8 us
    unnamed x1, local copies, waits for them, and re-layouts  2.04 us

profile of v3, /device:TPU:1, one launch (start us, length us, event | category | flops | bytes accessed | tf_op | source)
XLA Modules:
  0.0 85.8 jit_solution(3195198992209377388)
XLA Ops:
  0.0 83.8 %shard_map.109 = bf16[576,640]{1,0:T(8,128)(2,1)} custom-call(bf16[576,640]{1,0:T(8,128)(2,1)} %bitcast.7, bf16[18,640]{1,0:T(8,128)(2,1)} %refs.1, f32[640]{0:T(1024)} %norm_conv.1, bf16[3,3,640,640]{3,2,1,0:T(8,128)(2,1)} %conv_w.1, f32[640]{0:T(1024)} %norm_attn.1, bf16[3,640,640]{2,1,0:T(8,128)(2,1)} %sqkv.1, bf16[640,640]{1,0:T(8,128)(2,1)} %sout.1, ...), custom_call_target="tpu_custom_call" | custom-call | tf_op jit(solution)/shard_map/pallas_call | solution.py:551
  83.8 2.0 %copy.13 = bf16[1,16,36,640]{3,1,2,0:T(8,128)(2,1)} copy(bf16[1,16,36,640]{3,1,2,0:T(8,128)(2,1)} %bitcast.6) | data formatting | bytes 1474560

commit v4 on v3

--- a/solution.py
+++ b/solution.py
@@ -54,7 +54,7 @@
     rims, rimr, grid, mid,
     rblk, allx, wqt, wvt, wkp, qt, kk, vt, acc, mx, al, s0, s1,
     part, psend, precv,
-    asend, arecv, brecv, lsend, lrecv, lback, tgrid, tatt, oblk,
+    asend, arecv, brecv, lsend, lrecv, lback, into, outof, tgrid, tatt, oblk,
     lsem, hs, hr, cs, cr, p1s, p1r, p2s, p2r, xs, xr, ps, pr, a_s, a_r, b_s, b_r,
 ):
     f = lax.axis_index("frame")
@@ -162,6 +162,19 @@
     def conv_tap(b):
         return dot(grid[ROWS * b : ROWS * b + CELLS, :], wc[b])
 
+    few = LAST // FRAMES
+    slot_row = lax.broadcasted_iota(jnp.int32, (FRAMES * 16, LAST), 0)
+    cell = lax.broadcasted_iota(jnp.int32, (FRAMES * 16, LAST), 1)
+    slot_col = lax.broadcasted_iota(jnp.int32, (LAST, FRAMES * 16), 1)
+    cell_row = lax.broadcasted_iota(jnp.int32, (LAST, FRAMES * 16), 0)
+    for t in range(C // 128):
+        into[t] = jnp.where(
+            slot_row == (cell // few) * 16 + t * few + cell % few, 1.0, 0.0
+        ).astype(BF)
+        outof[t] = jnp.where(
+            slot_col == (cell_row // few) * 16 + t * few + cell_row % few, 1.0, 0.0
+        ).astype(BF)
+
     pl.semaphore_wait(bar, 13)
     up = remote(
         rims.at[pl.ds(0, 48)], rimr.at[pl.ds(48, 48)], hs.at[0], hr.at[0], (f, jnp.maximum(s - 1, 0))
@@ -355,37 +368,17 @@
         remote(psend.at[pl.ds(lo, n)], precv.at[pl.ds(lo, n)], ps.at[j], pr.at[j], sib)
         for j, (lo, n) in enumerate(PARTS)
     ]
-    few = LAST // FRAMES
     tall = FRAMES * 16
 
     def pack(values):
-        slot_row = lax.broadcasted_iota(jnp.int32, (tall, LAST), 0)
-        cell = lax.broadcasted_iota(jnp.int32, (tall, LAST), 1)
-        total = None
-        for t in range(C // 128):
-            want = slot_row - t * few
-            hit = jnp.logical_and(want % 16 < few, cell == (slot_row // 16) * few + want % 16)
-            hit = jnp.logical_and(hit, want % 16 == slot_row % 16 - t * few)
-            term = dot(jnp.where(hit, 1.0, 0.0).astype(BF), values[:, 128 * t : 128 * (t + 1)])
-            total = term if total is None else total + term
+        total = dot(into[0], values[:, :128])
+        for t in range(1, C // 128):
+            total += dot(into[t], values[:, 128 * t : 128 * (t + 1)])
         return total.reshape(FRAMES, 16, 128).astype(BF)
 
     def unpack(slots):
-        slot_row = lax.broadcasted_iota(jnp.int32, (LAST, tall), 1)
-        cell = lax.broadcasted_iota(jnp.int32, (LAST, tall), 0)
         flat = slots.reshape(tall, 128)
-        return jnp.concatenate(
-            [
-                dot(
-                    jnp.where(
-                        slot_row == (cell // few) * 16 + t * few + cell % few, 1.0, 0.0
-                    ).astype(BF),
-                    flat,
-                )
-                for t in range(C // 128)
-            ],
-            axis=1,
-        )
+        return jnp.concatenate([dot(outof[t], flat) for t in range(C // 128)], axis=1)
 
     hops = sorted(
         ((dx, dz, dy) for dx in range(4) for dz in range(2) for dy in range(4) if dx + dz + dy),
@@ -542,6 +535,7 @@
         v((CHUNKS - 1, FRAMES, SLOT, C), BF), v((CHUNKS - 1, FRAMES, SLOT, C), BF),
         v((CHUNKS - 1, FRAMES, SLOT, C), BF),
         v((FRAMES, 16, 128), BF), v((FRAMES, 16, 128), BF), v((FRAMES, 16, 128), BF),
+        v((C // 128, FRAMES * 16, LAST), BF), v((C // 128, LAST, FRAMES * 16), BF),
         v((WIDE, 3 * C), BF), v((WIDE, C), F32), v((CELLS, C), BF),
         dma((20,)), dma((2,)), dma((2,)), dma((7,)), dma((7,)),
         dma((3,)), dma((3,)), dma((4, 3)), dma((4, 3)), dma((5,)), dma((5,)), dma((3,)), dma((3,)),

time: 86 us -> 86.2 us (level)
  no operation moved by 1% of the time
where the time goes in v4:
time: 86.2 us; the launch traced here: 86.1 us
  Pallas kernels  84 us (97%)
  local copies, waits for them, and re-layouts  2.04 us (2%)
    pallas_call x1, Pallas kernels, block(): pl.pallas_call(kernel, out_shape=jax.ShapeDtypeStruct((CELLS, C), BF), in...  84 us
    unnamed x1, local copies, waits for them, and re-layouts  2.04 us

profile of v4, /device:TPU:1, one launch (start us, length us, event | category | flops | bytes accessed | tf_op | source)
XLA Modules:
  0.0 86.1 jit_solution(14788006128343644588)
XLA Ops:
  0.0 84.0 %shard_map.109 = bf16[576,640]{1,0:T(8,128)(2,1)} custom-call(bf16[576,640]{1,0:T(8,128)(2,1)} %bitcast.7, bf16[18,640]{1,0:T(8,128)(2,1)} %refs.1, f32[640]{0:T(1024)} %norm_conv.1, bf16[3,3,640,640]{3,2,1,0:T(8,128)(2,1)} %conv_w.1, f32[640]{0:T(1024)} %norm_attn.1, bf16[3,640,640]{2,1,0:T(8,128)(2,1)} %sqkv.1, bf16[640,640]{1,0:T(8,128)(2,1)} %sout.1, ...), custom_call_target="tpu_custom_call" | custom-call | tf_op jit(solution)/shard_map/pallas_call | solution.py:545
  84.0 2.0 %copy.13 = bf16[1,16,36,640]{3,1,2,0:T(8,128)(2,1)} copy(bf16[1,16,36,640]{3,1,2,0:T(8,128)(2,1)} %bitcast.6) | data formatting | bytes 1474560
